TPU v7x, 256 devices: a whole 4x4x8 slice. The times are simulated.
256 devices in a mesh: tm: 8 (over z_lo, y), space: 32 (over x, z_hi, core).
Axes of the slice: x: 4, y: 4, z: 8 (z_hi: 4, z_lo: 2; z = z_hi * 2 + z_lo), core: 2. Of those that a mesh axis runs over, the one named last changes fastest.
Arguments:
- video: bfloat16 [32, 256, 128, 128], P('tm', 'space'), may hold values from -10 to 10
- gain_first: float32 [128], replicated, may hold values from 0.1 to 1.9
- spatial_first: bfloat16 [9, 128, 128], replicated, may hold values from -0.1875 to 0.1875
- temporal_first: bfloat16 [3, 128, 128], replicated, may hold values from -0.3125 to 0.3125
- gain_second: float32 [128], replicated, may hold values from 0.1 to 1.9
- spatial_second: bfloat16 [9, 128, 128], replicated, may hold values from -0.1875 to 0.1875
- temporal_second: bfloat16 [3, 128, 128], replicated, may hold values from -0.3125 to 0.3125
Outputs:
- encoded: bfloat16 [32, 256, 128, 128], P('tm', 'space')
All inputs are finite; a program needn't handle non-finite values.
Results may differ from a plain program's by a relative error of at most 0.007.
Values may be sent and summed in bfloat16 or wider, within the bound.
A program may use at most 64 MiB of HBM per device.

v0:
```python
import jax
import jax.numpy as jnp
from jax import lax
from jax.sharding import PartitionSpec as P

G = 32


norm_eps = 1e-06


def with_halo(block, sides, width):
    for axis, dim in sides:
        count = lax.axis_size(axis)
        forward = [(i, i + 1) for i in range(count - 1)]
        backward = [(target, source) for source, target in forward]
        low = lax.ppermute(
            lax.slice_in_dim(block, block.shape[dim] - width, None, axis=dim), axis, forward
        )
        high = lax.ppermute(lax.slice_in_dim(block, 0, width, axis=dim), axis, backward)
        block = jnp.concatenate([low, block, high], axis=dim)
    return block


def passed_along(value, axis, steps):
    count = lax.axis_size(axis)
    leading, last = (max(0, -steps), min(count, count - steps))
    return lax.ppermute(value, axis, [(source, source + steps) for source in range(leading, last)])


def frame_moments(values):
    frames, tile_rows, tile_cols, channels = values.shape
    per_group = channels // G
    as_float = values.astype(jnp.float32)
    totals = jnp.sum(as_float, axis=(1, 2)).reshape(frames, G, per_group).sum(axis=2)
    squares = jnp.sum(as_float * as_float, axis=(1, 2)).reshape(frames, G, per_group).sum(axis=2)
    totals, squares = lax.psum((totals, squares), "space")
    members = tile_rows * lax.axis_size("space") * tile_cols * per_group
    center = totals / members
    inverse = lax.rsqrt(squares / members - center * center + norm_eps)
    return (jnp.repeat(center, per_group, axis=1), jnp.repeat(inverse, per_group, axis=1))


def activate(values, center, inverse, gain):
    normed = (
        (values.astype(jnp.float32) - center[:, None, None, :]) * inverse[:, None, None, :] * gain
    )
    return jax.nn.silu(normed).astype(jnp.bfloat16)


def padded_input(values, gain):
    center, inverse = frame_moments(values)
    return with_halo(activate(values, center, inverse, gain), (("space", 1),), 1)


def spatial_conv(bordered, weight):
    frames, wide_rows, tile_cols, channels = bordered.shape
    tile_rows = wide_rows - 2
    padded = jnp.pad(bordered, ((0, 0), (0, 0), (1, 1), (0, 0)))
    total = jnp.zeros((frames, tile_rows, tile_cols, channels), jnp.float32)
    for row_shift in range(3):
        for col_shift in range(3):
            window = padded[
                :, row_shift : row_shift + tile_rows, col_shift : col_shift + tile_cols, :
            ]
            total = total + jnp.dot(
                window, weight[3 * row_shift + col_shift], preferred_element_type=jnp.float32
            )
    return total.astype(jnp.bfloat16)


def extended_frames(bordered, weight):
    mixed = spatial_conv(bordered, weight)
    earlier = passed_along(mixed[-2:], "tm", 1)
    opening = jnp.concatenate([mixed[:1], mixed[:1]], axis=0)
    earlier = jnp.where(lax.axis_index("tm") == 0, opening, earlier)
    return jnp.concatenate([earlier, mixed], axis=0)


def temporal_conv(extended, weight):
    frames = extended.shape[0] - 2
    total = jnp.dot(extended[0:frames], weight[0], preferred_element_type=jnp.float32)
    for offset in range(1, 3):
        total = total + jnp.dot(
            extended[offset : offset + frames], weight[offset], preferred_element_type=jnp.float32
        )
    return total


def shards(
    video, gain_first, spatial_first, temporal_first, gain_second, spatial_second, temporal_second
):
    bordered_first = padded_input(video, gain_first)
    extended_first = extended_frames(bordered_first, spatial_first)
    hidden = temporal_conv(extended_first, temporal_first).astype(jnp.bfloat16)
    bordered_second = padded_input(hidden, gain_second)
    extended_second = extended_frames(bordered_second, spatial_second)
    result = video.astype(jnp.float32) + temporal_conv(extended_second, temporal_second)
    return result.astype(jnp.bfloat16)


def solution(mesh):
    in_specs = (P("tm", "space", None, None), P(), P(), P(), P(), P(), P())
    out_specs = P("tm", "space", None, None)
    return jax.shard_map(shards, mesh=mesh, in_specs=in_specs, out_specs=out_specs, check_vma=False)
```

profile of v0, /device:TPU:25, one launch (start us, length us, event | category | flops | bytes accessed | tf_op | source)
XLA Modules:
  0.0 208.6 jit_solution(11449095192430447798)
XLA Ops:
  0.0 1.6 convert_reduce_fusion
  1.6 0.1 reshape.18
  1.7 0.1 reshape.19
  2.0 72.5 %all-reduce.3 = (f32[4,32]{1,0:T(4,128)S(1)}, f32[4,32]{1,0:T(4,128)S(1)}) all-reduce(f32[4,32]{1,0:T(4,128)S(1)} %reduce_sum.75, f32[4,32]{1,0:T(4,128)S(1)} %reduce_sum.73), channel_id=1, replica_groups=mesh['tm'=8,'space'=32] {'space'}, use_global_device_ids=true, to_apply=%region_5.0 | all-reduce | flops 256 | bytes 2048 | tf_op jit(solution)/shard_map/psum | solution.py:37
  74.7 0.1 sub.26
  74.9 0.1 mul.57
  75.0 1.3 fusion.17
  76.4 3.9 %collective-permute-start = (bf16[4,1,128,128]{3,2,1,0:T(8,128)(2,1)S(1)}, bf16[4,1,128,128]{3,2,1,0:T(8,128)(2,1)S(1)}, u32[]{:S(2)}, u32[]{:S(2)}) collective-permute-start(bf16[4,1,128,128]{3,2,1,0:T(8,128)(2,1)S(1)} %get-tuple-element.15), channel_id=1, source_target_pairs={{0,1},{1,2},{2,3},{3,4},{4,5},{5,6},{6,7},{7,8},{8,9},{9,10},{10,1... | collective-permute-start | bytes 393224 | tf_op jit(solution)/shard_map/ppermute | solution.py:17
  80.3 5.2 %collective-permute-start.1 = (bf16[4,1,128,128]{3,2,1,0:T(8,128)(2,1)S(1)}, bf16[4,1,128,128]{3,2,1,0:T(8,128)(2,1)S(1)}, u32[]{:S(2)}, u32[]{:S(2)}) collective-permute-start(bf16[4,1,128,128]{3,2,1,0:T(8,128)(2,1)S(1)} %get-tuple-element.16), channel_id=1, source_target_pairs={{1,0},{2,1},{3,2},{4,3},{5,4},{6,5},{7,6},{8,7},{9,8},{10,9},{11,1... | collective-permute-start | bytes 393224 | tf_op jit(solution)/shard_map/ppermute | solution.py:20
  85.5 0.4 fusion.93
  86.0 2.9 %collective-permute-done.1 = bf16[4,1,128,128]{3,2,1,0:T(8,128)(2,1)S(1)} collective-permute-done((bf16[4,1,128,128]{3,2,1,0:T(8,128)(2,1)S(1)}, bf16[4,1,128,128]{3,2,1,0:T(8,128)(2,1)S(1)}, u32[]{:S(2)}, u32[]{:S(2)}) %collective-permute-start.1) | collective-permute-done | bytes 131104 | tf_op jit(solution)/shard_map/ppermute | solution.py:20
  88.9 0.6 fusion.24
  89.5 0.4 fusion.59
  89.9 0.4 fusion.61
  90.3 0.4 fusion.63
  90.7 0.4 fusion.65
  91.2 0.4 fusion.67
  91.6 0.4 fusion.25
  92.0 0.4 fusion.29
  92.4 1.0 add_convert_fusion.2
  93.5 1.9 collective-permute-start.2
  95.5 0.4 fusion.85
  95.9 11.6 %collective-permute-done.2 = bf16[2,8,128,128]{3,2,1,0:T(8,128)(2,1)S(1)} collective-permute-done((bf16[2,8,128,128]{3,2,1,0:T(8,128)(2,1)S(1)}, bf16[2,8,128,128]{3,2,1,0:T(8,128)(2,1)S(1)}, u32[]{:S(2)}, u32[]{:S(2)}) %collective-permute-start.2) | collective-permute-done | bytes 524320 | tf_op jit(solution)/shard_map/ppermute | solution.py:28
  107.6 0.4 fusion.70
  108.1 0.7 convert_reduce_fusion.1
  108.9 0.1 reshape.21
  109.1 68.3 %all-reduce.2 = (f32[4,32]{1,0:T(4,128)S(1)}, f32[4,32]{1,0:T(4,128)S(1)}) all-reduce(f32[4,32]{1,0:T(4,128)S(1)} %reduce_sum.79, f32[4,32]{1,0:T(4,128)S(1)} %reduce_sum.77), channel_id=1, replica_groups=mesh['tm'=8,'space'=32] {'space'}, use_global_device_ids=true, to_apply=%region_11.12 | all-reduce | flops 256 | bytes 2048 | tf_op jit(solution)/shard_map/psum | solution.py:37
  177.5 0.1 sub.30
  177.7 0.1 mul.65
  177.8 0.7 fusion.8
  178.6 1.9 collective-permute-start.3
  180.5 3.5 %collective-permute-start.4 = (bf16[4,1,128,128]{3,2,1,0:T(8,128)(2,1)S(1)}, bf16[4,1,128,128]{3,2,1,0:T(8,128)(2,1)S(1)}, u32[]{:S(2)}, u32[]{:S(2)}) collective-permute-start(bf16[4,1,128,128]{3,2,1,0:T(8,128)(2,1)S(1)} %get-tuple-element.14), channel_id=1, source_target_pairs={{1,0},{2,1},{3,2},{4,3},{5,4},{6,5},{7,6},{8,7},{9,8},{10,9},{11,1... | collective-permute-start | bytes 393224 | tf_op jit(solution)/shard_map/ppermute | solution.py:20
  184.1 0.4 fusion.79
  184.5 4.6 %collective-permute-done.4 = bf16[4,1,128,128]{3,2,1,0:T(8,128)(2,1)S(1)} collective-permute-done((bf16[4,1,128,128]{3,2,1,0:T(8,128)(2,1)S(1)}, bf16[4,1,128,128]{3,2,1,0:T(8,128)(2,1)S(1)}, u32[]{:S(2)}, u32[]{:S(2)}) %collective-permute-start.4) | collective-permute-done | bytes 131104 | tf_op jit(solution)/shard_map/ppermute | solution.py:20
  189.1 0.6 select_maximum_fusion
  189.7 0.4 fusion.45
  190.1 0.4 fusion.47
  190.5 0.4 fusion.49
  191.0 0.4 fusion.51
  191.4 0.4 fusion.53
  191.8 0.4 fusion.33
  192.2 0.4 fusion.37
  192.7 1.0 add_convert_fusion
  193.8 3.4 %collective-permute-start.5 = (bf16[2,8,128,128]{3,2,1,0:T(8,128)(2,1)S(1)}, bf16[2,8,128,128]{3,2,1,0:T(8,128)(2,1)S(1)}, u32[]{:S(2)}, u32[]{:S(2)}) collective-permute-start(bf16[2,8,128,128]{3,2,1,0:T(8,128)(2,1)S(1)} %slice.241), channel_id=1, source_target_pairs={{0,32},{32,64},{64,96},{96,128},{128,160},{160,192},{192,224},{1,3... | collective-permute-start | bytes 1572872 | tf_op jit(solution)/shard_map/ppermute | solution.py:28
  197.2 0.4 fusion.71
  197.6 8.9 %collective-permute-done.5 = bf16[2,8,128,128]{3,2,1,0:T(8,128)(2,1)S(1)} collective-permute-done((bf16[2,8,128,128]{3,2,1,0:T(8,128)(2,1)S(1)}, bf16[2,8,128,128]{3,2,1,0:T(8,128)(2,1)S(1)}, u32[]{:S(2)}, u32[]{:S(2)}) %collective-permute-start.5) | collective-permute-done | bytes 524320 | tf_op jit(solution)/shard_map/ppermute | solution.py:28
  206.6 0.4 fusion.69
  207.0 1.6 fusion.19
  (33 shorter events, 1.1 us)
Async XLA Ops:
  0.0 75.0 %copy-start = (bf16[4,8,128,128]{3,2,1,0:T(8,128)(2,1)S(1)}, bf16[4,8,128,128]{3,2,1,0:T(8,128)(2,1)}, u32[]{:S(2)}) copy-start(bf16[4,8,128,128]{3,2,1,0:T(8,128)(2,1)} %param.7) | copy-start | bytes 3145732
  0.0 85.5 %copy-start.1 = (bf16[9,128,128]{2,1,0:T(8,128)(2,1)S(1)}, bf16[9,128,128]{2,1,0:T(8,128)(2,1)}, u32[]{:S(2)}) copy-start(bf16[9,128,128]{2,1,0:T(8,128)(2,1)} %param.9) | copy-start | bytes 884740
  76.4 9.6 %collective-permute-start = (bf16[4,1,128,128]{3,2,1,0:T(8,128)(2,1)S(1)}, bf16[4,1,128,128]{3,2,1,0:T(8,128)(2,1)S(1)}, u32[]{:S(2)}, u32[]{:S(2)}) collective-permute-start(bf16[4,1,128,128]{3,2,1,0:T(8,128)(2,1)S(1)} %get-tuple-element.15), channel_id=1, source_target_pairs={{0,1},{1,2},{2,3},{3,4},{4,5},{5,6},{6,7},{7,8},{8,9},{9,10},{10,1... | collective-permute-start | bytes 393224 | tf_op jit(solution)/shard_map/ppermute | solution.py:17
  80.3 8.6 %collective-permute-start.1 = (bf16[4,1,128,128]{3,2,1,0:T(8,128)(2,1)S(1)}, bf16[4,1,128,128]{3,2,1,0:T(8,128)(2,1)S(1)}, u32[]{:S(2)}, u32[]{:S(2)}) collective-permute-start(bf16[4,1,128,128]{3,2,1,0:T(8,128)(2,1)S(1)} %get-tuple-element.16), channel_id=1, source_target_pairs={{1,0},{2,1},{3,2},{4,3},{5,4},{6,5},{7,6},{8,7},{9,8},{10,9},{11,1... | collective-permute-start | bytes 393224 | tf_op jit(solution)/shard_map/ppermute | solution.py:20
  92.4 3.1 %copy-start.3 = (bf16[3,128,128]{2,1,0:T(8,128)(2,1)S(1)}, bf16[3,128,128]{2,1,0:T(8,128)(2,1)}, u32[]{:S(2)}) copy-start(bf16[3,128,128]{2,1,0:T(8,128)(2,1)} %param.10) | copy-start | bytes 294916
  93.5 14.0 %collective-permute-start.2 = (bf16[2,8,128,128]{3,2,1,0:T(8,128)(2,1)S(1)}, bf16[2,8,128,128]{3,2,1,0:T(8,128)(2,1)S(1)}, u32[]{:S(2)}, u32[]{:S(2)}) collective-permute-start(bf16[2,8,128,128]{3,2,1,0:T(8,128)(2,1)S(1)} %slice.231), channel_id=1, source_target_pairs={{0,32},{32,64},{64,96},{96,128},{128,160},{160,192},{192,224},{1,3... | collective-permute-start | bytes 1572872 | tf_op jit(solution)/shard_map/ppermute | solution.py:28
  108.0 69.8 %copy-start.5 = (f32[128]{0:T(128)S(1)}, f32[128]{0:T(128)}, u32[]{:S(2)}) copy-start(f32[128]{0:T(128)} %param.11) | copy-start | bytes 1540
  108.7 75.3 %copy-start.2 = (bf16[9,128,128]{2,1,0:T(8,128)(2,1)S(1)}, bf16[9,128,128]{2,1,0:T(8,128)(2,1)}, u32[]{:S(2)}) copy-start(bf16[9,128,128]{2,1,0:T(8,128)(2,1)} %param.12) | copy-start | bytes 884740
  178.6 5.9 %collective-permute-start.3 = (bf16[4,1,128,128]{3,2,1,0:T(8,128)(2,1)S(1)}, bf16[4,1,128,128]{3,2,1,0:T(8,128)(2,1)S(1)}, u32[]{:S(2)}, u32[]{:S(2)}) collective-permute-start(bf16[4,1,128,128]{3,2,1,0:T(8,128)(2,1)S(1)} %get-tuple-element.13), channel_id=1, source_target_pairs={{0,1},{1,2},{2,3},{3,4},{4,5},{5,6},{6,7},{7,8},{8,9},{9,10},{10,1... | collective-permute-start | bytes 393224 | tf_op jit(solution)/shard_map/ppermute | solution.py:17
  180.5 8.6 %collective-permute-start.4 = (bf16[4,1,128,128]{3,2,1,0:T(8,128)(2,1)S(1)}, bf16[4,1,128,128]{3,2,1,0:T(8,128)(2,1)S(1)}, u32[]{:S(2)}, u32[]{:S(2)}) collective-permute-start(bf16[4,1,128,128]{3,2,1,0:T(8,128)(2,1)S(1)} %get-tuple-element.14), channel_id=1, source_target_pairs={{1,0},{2,1},{3,2},{4,3},{5,4},{6,5},{7,6},{8,7},{9,8},{10,9},{11,1... | collective-permute-start | bytes 393224 | tf_op jit(solution)/shard_map/ppermute | solution.py:20
  192.7 4.5 %copy-start.4 = (bf16[3,128,128]{2,1,0:T(8,128)(2,1)S(1)}, bf16[3,128,128]{2,1,0:T(8,128)(2,1)}, u32[]{:S(2)}) copy-start(bf16[3,128,128]{2,1,0:T(8,128)(2,1)} %param.13) | copy-start | bytes 294916
  193.8 12.7 %collective-permute-start.5 = (bf16[2,8,128,128]{3,2,1,0:T(8,128)(2,1)S(1)}, bf16[2,8,128,128]{3,2,1,0:T(8,128)(2,1)S(1)}, u32[]{:S(2)}, u32[]{:S(2)}) collective-permute-start(bf16[2,8,128,128]{3,2,1,0:T(8,128)(2,1)S(1)} %slice.241), channel_id=1, source_target_pairs={{0,32},{32,64},{64,96},{96,128},{128,160},{160,192},{192,224},{1,3... | collective-permute-start | bytes 1572872 | tf_op jit(solution)/shard_map/ppermute | solution.py:28
where the time goes:
time: 212 us; the launch traced here: 209 us
  blocking collectives  141 us (67%)
  waiting for transfers between devices  28 us (13%)
  starting transfers between devices  19.9 us (9%)
  matrix products  12.7 us (6%)
  other arithmetic  5.38 us (3%)
    psum x2, blocking collectives, frame_moments(): totals, squares = lax.psum((totals, squares), 'space')  141 us
    ppermute x2, waiting for transfers between devices, passed_along(): lax.ppermute(value, axis, [(source, source + steps) for source in range(l...  20.5 us
    dot_general x18, matrix products, spatial_conv(): jnp.dot(window, weight[3 * row_shift + col_shift], preferred_element_type...  8.84 us
    ppermute x2, starting transfers between devices, with_halo(): lax.ppermute(lax.slice_in_dim(block, 0, width, axis=dim), axis, backward)  8.8 us
    ppermute x2, waiting for transfers between devices, with_halo(): lax.ppermute(lax.slice_in_dim(block, 0, width, axis=dim), axis, backward)  7.48 us
    ppermute x2, starting transfers between devices, with_halo(): lax.ppermute(lax.slice_in_dim(block, block.shape[dim] - width, None, axis...  5.8 us
    ppermute x2, starting transfers between devices, passed_along(): lax.ppermute(value, axis, [(source, source + steps) for source in range(l...  5.32 us
  transfers between devices with their start and end apart: 6, of which 4 were waited for; matrix products, arithmetic and copies ran while one was open for 1% of the time, Pallas kernels for 0%

commit v1 on v0

v1 whole, which is shorter than its diff:
```python
import jax
import jax.numpy as jnp
from jax import lax
from jax.experimental import pallas as pl
from jax.experimental.pallas import tpu as pltpu
from jax.sharding import PartitionSpec as P

G = 32
C = 128
norm_eps = 1e-06

F32 = jnp.float32
BF16 = jnp.bfloat16

PARTS = 2


def kernel(
    members,
    video, gain1, sp1, tp1, gain2, sp2, tp2, out,
    xin, act, s1, s2, hid, w1, w2, t1, t2, g1, g2, outb, st_send, st_recv,
    ld_sem, w_sem, st_ssem, st_rsem, h_ssem, h_rsem, s_ssem, s_rsem, out_sem,
):
    frames, rows, cols, _ = video.shape
    pairs = rows // 2
    n_space, n_tm = lax.axis_size("space"), lax.axis_size("tm")
    space, tm = lax.axis_index("space"), lax.axis_index("tm")
    has_up, has_down = space > 0, space < n_space - 1
    has_before, has_after = tm > 0, tm < n_tm - 1
    others = n_space - 1

    barrier = pltpu.get_barrier_semaphore()

    def greet(d, _):
        pl.semaphore_signal(barrier, 1, device_id={"space": lax.rem(space + d, n_space)})
        return 0

    lax.fori_loop(1, n_space, greet, 0)

    @pl.when(has_before)
    def _():
        pl.semaphore_signal(barrier, 1, device_id={"tm": tm - 1})

    @pl.when(has_after)
    def _():
        pl.semaphore_signal(barrier, 1, device_id={"tm": tm + 1})

    loads = [
        pltpu.make_async_copy(video.at[f], xin.at[f, pl.ds(1, rows)], ld_sem.at[f])
        for f in range(frames)
    ]
    for load in loads:
        load.start()
    weight_loads = [
        pltpu.make_async_copy(gain1, g1, w_sem.at[0]),
        pltpu.make_async_copy(sp1, w1.at[pl.ds(0, 9), :, pl.ds(0, C)], w_sem.at[1]),
        pltpu.make_async_copy(sp1, w1.at[pl.ds(3, 9), :, pl.ds(C, C)], w_sem.at[2]),
        pltpu.make_async_copy(tp1, t1.at[pl.ds(0, 3), :, pl.ds(0, C)], w_sem.at[3]),
        pltpu.make_async_copy(tp1, t1.at[pl.ds(1, 3), :, pl.ds(C, C)], w_sem.at[4]),
        pltpu.make_async_copy(gain2, g2, w_sem.at[5]),
        pltpu.make_async_copy(sp2, w2.at[pl.ds(0, 9), :, pl.ds(0, C)], w_sem.at[6]),
        pltpu.make_async_copy(sp2, w2.at[pl.ds(3, 9), :, pl.ds(C, C)], w_sem.at[7]),
        pltpu.make_async_copy(tp2, t2.at[pl.ds(0, 3), :, pl.ds(0, C)], w_sem.at[8]),
        pltpu.make_async_copy(tp2, t2.at[pl.ds(1, 3), :, pl.ds(C, C)], w_sem.at[9]),
    ]
    for load in weight_loads:
        load.start()
    for w in (w1, w2):
        w[pl.ds(9, 3), :, pl.ds(0, C)] = jnp.zeros((3, C, C), BF16)
        w[pl.ds(0, 3), :, pl.ds(C, C)] = jnp.zeros((3, C, C), BF16)
    for t in (t1, t2):
        t[pl.ds(3, 1), :, pl.ds(0, C)] = jnp.zeros((1, C, C), BF16)
        t[pl.ds(0, 1), :, pl.ds(C, C)] = jnp.zeros((1, C, C), BF16)

    def moments(x):
        x = x.reshape(-1, 8, C)
        return (
            jnp.sum(jnp.sum(x, axis=0), axis=0, keepdims=True),
            jnp.sum(jnp.sum(x * x, axis=0), axis=0, keepdims=True),
        )

    def exchange(k):
        def send(d, _):
            pltpu.make_async_remote_copy(
                st_send.at[k],
                st_recv.at[k, d - 1],
                st_ssem.at[k],
                st_rsem.at[k],
                device_id={"space": lax.rem(space + d, n_space)},
            ).start()
            return 0

        lax.fori_loop(1, n_space, send, 0)

    def all_sums(k):
        whole = st_recv.at[k, pl.ds(0, others)]
        pltpu.make_async_copy(whole, whole, st_rsem.at[k]).wait()
        total = st_send[k] + jnp.sum(st_recv[k], axis=0)
        lane = lax.broadcasted_iota(jnp.int32, (8, C), 1)
        size = C // G
        step = 1
        while step < size:
            low = lax.rem(lane, 2 * step) < step
            total = total + jnp.where(
                low, pltpu.roll(total, C - step, 1), pltpu.roll(total, step, 1)
            )
            step *= 2
        return total

    def scales(total, n, gain):
        center = total[0:n] / members
        inverse = lax.rsqrt(total[n : 2 * n] / members - center * center + norm_eps)
        return center, inverse * gain * 0.5

    first_col = lax.broadcasted_iota(jnp.int32, (cols, C), 0) == 0
    last_col = lax.broadcasted_iota(jnp.int32, (cols, C), 0) == cols - 1

    def activate(src, f, q, center, half):
        h = (src[f, q].astype(F32) - center) * half
        a = h * (1.0 + jnp.tanh(h))
        left = jnp.where(first_col, 0.0, pltpu.roll(a, 1, 0))
        right = jnp.where(last_col, 0.0, pltpu.roll(a, cols - 1, 0))
        act[f, q // 2, q % 2, :, pl.ds(0, C)] = left.astype(BF16)
        act[f, q // 2, q % 2, :, pl.ds(C, C)] = a.astype(BF16)
        act[f, q // 2, q % 2, :, pl.ds(2 * C, C)] = right.astype(BF16)

    def activate_tile(src, f, center, half):
        def step(p, _):
            for o in (1, 2):
                activate(src, f, 2 * p + o, center, half)
            return 0

        lax.fori_loop(0, pairs, step, 0)

    def halo_copies(k, src, src_up, src_down, dst, lo, n):
        up = pltpu.make_async_remote_copy(
            src.at[pl.ds(lo, n), src_up],
            dst.at[pl.ds(lo, n), rows + 1],
            h_ssem.at[k, 0],
            h_rsem.at[k, 0],
            device_id={"space": lax.max(space - 1, 0)},
        )
        down = pltpu.make_async_remote_copy(
            src.at[pl.ds(lo, n), src_down],
            dst.at[pl.ds(lo, n), 0],
            h_ssem.at[k, 1],
            h_rsem.at[k, 1],
            device_id={"space": lax.min(space + 1, n_space - 1)},
        )
        return up, down

    def send_halo(copies):
        up, down = copies

        @pl.when(has_up)
        def _():
            up.start()

        @pl.when(has_down)
        def _():
            down.start()

    def wait_halo_in(copies):
        up, down = copies

        @pl.when(has_down)
        def _():
            up.wait_recv()

        @pl.when(has_up)
        def _():
            down.wait_recv()

    def wait_halo_out(copies):
        up, down = copies

        @pl.when(has_up)
        def _():
            up.wait_send()

        @pl.when(has_down)
        def _():
            down.wait_send()

    def activate_halo(src, fs):
        for present, q in ((has_up, 0), (has_down, rows + 1)):

            @pl.when(present)
            def _():
                for f, center, half in fs:
                    activate(src, f, q, center, half)

            @pl.when(jnp.logical_not(present))
            def _():
                for f, _c, _h in fs:
                    act[f, q // 2, q % 2] = jnp.zeros((cols, 3 * C), BF16)

    np_ = pairs // PARTS

    def spatial(w, s, f0, part):
        p0 = part * np_
        lhs = jnp.concatenate(
            [
                act[pl.ds(f0, 2), pl.ds(p0 + i // 2, np_), i % 2].reshape(2 * np_ * cols, 3 * C)
                for i in range(4)
            ],
            axis=1,
        )
        o = jnp.dot(lhs, w[...].reshape(12 * C, 2 * C), preferred_element_type=F32)
        o = o.astype(BF16).reshape(2, np_, cols, 2 * C)
        s[pl.ds(2 + f0, 2), pl.ds(p0, np_), 0] = o[..., :C]
        s[pl.ds(2 + f0, 2), pl.ds(p0, np_), 1] = o[..., C:]

    def temporal(t, s, f0, part):
        p0 = part * np_
        lhs = jnp.concatenate(
            [s[f0 + i, pl.ds(p0, np_)].reshape(2 * np_ * cols, C) for i in range(4)], axis=1
        )
        return jnp.dot(lhs, t[...].reshape(4 * C, 2 * C), preferred_element_type=F32)

    def carry_copy(k, s, part):
        here = pl.ds(part * np_, np_)
        return pltpu.make_async_remote_copy(
            s.at[pl.ds(frames, 2), here],
            s.at[pl.ds(0, 2), here],
            s_ssem.at[k, part],
            s_rsem.at[k, part],
            device_id={"tm": lax.min(tm + 1, n_tm - 1)},
        )

    def carry(k, s, part):
        copy = carry_copy(k, s, part)

        @pl.when(has_after)
        def _():
            copy.start()

    def carried(k, s, part):
        copy = carry_copy(k, s, part)

        @pl.when(has_before)
        def _():
            copy.wait_recv()

        @pl.when(jnp.logical_not(has_before))
        def _():
            here = pl.ds(part * np_, np_)
            s[0, here] = s[2, here]
            s[1, here] = s[2, here]

    def hidden_part(f0, part):
        h = temporal(t1, s1, f0, part).astype(BF16)
        own = pl.ds(1 + part * 2 * np_, 2 * np_)
        sums = []
        for j in range(2):
            hj = h[:, j * C : (j + 1) * C]
            hid[f0 + j, own] = hj.reshape(2 * np_, cols, C)
            sums.append(moments(hj.astype(F32)))
        return [sums[0][0], sums[1][0], sums[0][1], sums[1][1]]

    def hidden(k, f0):
        sums = None
        for part in range(PARTS):
            if f0 == 0:
                carried(0, s1, part)
            new = hidden_part(f0, part)
            sums = new if sums is None else [a + b for a, b in zip(sums, new)]
        st_send[k] = jnp.concatenate(sums + [jnp.zeros((4, C), F32)], axis=0)
        exchange(k)
        copies = halo_copies(k, hid, 1, rows, hid, f0, 2)
        send_halo(copies)
        return copies

    def second(k, f0, copies):
        center, half = scales(all_sums(k), 2, g2[...].reshape(1, C))
        fs = [(f0 + j, center[j : j + 1], half[j : j + 1]) for j in range(2)]
        for f in fs:
            activate_tile(hid, *f)
        wait_halo_in(copies)
        activate_halo(hid, fs)

    out_copies = []

    def finish(f0, part):
        r = temporal(t2, s2, f0, part)
        rows_here = 2 * np_
        r0 = part * rows_here
        for j in range(2):
            v = xin[f0 + j, pl.ds(1 + r0, rows_here)].astype(F32)
            total = v + r[:, j * C : (j + 1) * C].reshape(rows_here, cols, C)
            outb[f0 + j, pl.ds(r0, rows_here)] = total.astype(BF16)
        here = (pl.ds(f0, 2), pl.ds(r0, rows_here))
        copy = pltpu.make_async_copy(outb.at[here], out.at[here], out_sem.at[f0 // 2, part])
        copy.start()
        out_copies.append(copy)

    sums = []
    for f in range(frames):
        loads[f].wait()

        def add(p, c, f=f):
            x = xin[f, pl.ds(1 + 2 * p, 2)].astype(F32).reshape(-1, 8, C)
            return c[0] + jnp.sum(x, axis=0), c[1] + jnp.sum(x * x, axis=0)

        zero = jnp.zeros((8, C), F32)
        a, b = lax.fori_loop(0, pairs, add, (zero, zero))
        sums.append((jnp.sum(a, axis=0, keepdims=True), jnp.sum(b, axis=0, keepdims=True)))
    st_send[0] = jnp.concatenate([s[0] for s in sums] + [s[1] for s in sums], axis=0)

    greeted = others + has_before.astype(jnp.int32) + has_after.astype(jnp.int32)
    pl.semaphore_wait(barrier, greeted)
    exchange(0)
    halo0 = halo_copies(0, video, 0, rows - 1, xin, 0, frames)
    send_halo(halo0)

    for load in weight_loads:
        load.wait()
    center, half = scales(all_sums(0), 4, g1[...].reshape(1, C))
    fs = [(f, center[f : f + 1], half[f : f + 1]) for f in range(frames)]
    for f in (2, 3):
        activate_tile(xin, *fs[f])
    wait_halo_in(halo0)
    activate_halo(xin, fs)
    for part in range(PARTS):
        spatial(w1, s1, 2, part)
        carry(0, s1, part)
    for f in (0, 1):
        activate_tile(xin, *fs[f])
    for part in range(PARTS):
        spatial(w1, s1, 0, part)

    halo1 = hidden(1, 2)
    second(1, 2, halo1)
    for part in range(PARTS):
        spatial(w2, s2, 2, part)
        carry(1, s2, part)

    halo2 = hidden(2, 0)
    second(2, 0, halo2)
    for part in range(PARTS):
        spatial(w2, s2, 0, part)
    for part in range(PARTS):
        finish(2, part)
    for part in range(PARTS):
        carried(1, s2, part)
        finish(0, part)

    for k, copies in enumerate((halo0, halo1, halo2)):
        wait_halo_out(copies)
        whole = st_recv.at[k, pl.ds(0, others)]
        pltpu.make_async_copy(whole, whole, st_ssem.at[k]).wait()
    for k, s in ((0, s1), (1, s2)):
        for part in range(PARTS):
            copy = carry_copy(k, s, part)

            @pl.when(has_after)
            def _():
                copy.wait_send()
    for copy in out_copies:
        copy.wait()


def shards(video, gain1, sp1, tp1, gain2, sp2, tp2):
    frames, rows, cols, channels = video.shape
    n_space = lax.axis_size("space")
    members = rows * n_space * cols * (channels // G)
    any_spec = pl.BlockSpec(memory_space=pl.ANY)
    call = pl.pallas_call(
        lambda *refs: kernel(float(members), *refs),
        out_shape=jax.ShapeDtypeStruct(video.shape, BF16),
        in_specs=[any_spec] * 7,
        out_specs=any_spec,
        scratch_shapes=[
            pltpu.VMEM((frames, rows + 2, cols, C), BF16),
            pltpu.VMEM((frames, rows // 2 + 1, 2, cols, 3 * C), BF16),
            pltpu.VMEM((frames + 2, rows // 2, 2, cols, C), BF16),
            pltpu.VMEM((frames + 2, rows // 2, 2, cols, C), BF16),
            pltpu.VMEM((frames, rows + 2, cols, C), BF16),
            pltpu.VMEM((12, C, 2 * C), BF16),
            pltpu.VMEM((12, C, 2 * C), BF16),
            pltpu.VMEM((4, C, 2 * C), BF16),
            pltpu.VMEM((4, C, 2 * C), BF16),
            pltpu.VMEM((C,), F32),
            pltpu.VMEM((C,), F32),
            pltpu.VMEM((frames, rows, cols, C), BF16),
            pltpu.VMEM((3, 8, C), F32),
            pltpu.VMEM((3, n_space - 1, 8, C), F32),
            pltpu.SemaphoreType.DMA((frames,)),
            pltpu.SemaphoreType.DMA((10,)),
            pltpu.SemaphoreType.DMA((3,)),
            pltpu.SemaphoreType.DMA((3,)),
            pltpu.SemaphoreType.DMA((3, 2)),
            pltpu.SemaphoreType.DMA((3, 2)),
            pltpu.SemaphoreType.DMA((2, PARTS)),
            pltpu.SemaphoreType.DMA((2, PARTS)),
            pltpu.SemaphoreType.DMA((2, PARTS)),
        ],
        compiler_params=pltpu.CompilerParams(
            collective_id=0, has_side_effects=True, vmem_limit_bytes=48 * 2**20
        ),
        cost_estimate=pl.CostEstimate(
            flops=4 * 10**9, bytes_accessed=4 * 2**20, transcendentals=10**6
        ),
        name="block",
    )
    return call(video, gain1, sp1, tp1, gain2, sp2, tp2)


def solution(mesh):
    in_specs = (P("tm", "space", None, None), P(), P(), P(), P(), P(), P())
    out_specs = P("tm", "space", None, None)
    return jax.shard_map(shards, mesh=mesh, in_specs=in_specs, out_specs=out_specs, check_vma=False)
```

time: 212 us -> 70.3 us (0.33); the launches traced: 209 us -> 70 us
  blocking collectives: 141 us -> 0 us
  Pallas kernels: 0 us -> 62.8 us
  waiting for transfers between devices: 28 us -> 0 us
  starting transfers between devices: 19.9 us -> 0 us
  matrix products: 12.7 us -> 0 us
  local copies, waits for them, and re-layouts: 1.38 us -> 7.21 us
  other arithmetic: 5.38 us -> 0 us
    psum x2 -> x0, blocking collectives: 141 us -> none  [frame_moments(): totals, squares = lax.psum((totals, squares), 'space')]
    pallas_call x0 -> x1, Pallas kernels: none -> 62.8 us  [shards(): return call(video, gain1, sp1, tp1, gain2, sp2, tp2)]
    ppermute x6 -> x0, waiting for transfers between devices: 28 us -> none  [the longest x2 20.5 us: passed_along(): lax.ppermute(value, axis, [(source, source + steps) for source in range(l...]
    ppermute x6 -> x0, starting transfers between devices: 19.9 us -> none  [the longest x2 8.8 us: with_halo(): lax.ppermute(lax.slice_in_dim(block, 0, width, axis=dim), axis, backward)]
    dot_general x24 -> x0, matrix products: 12.7 us -> none  [the longest x18 8.84 us: spatial_conv(): jnp.dot(window, weight[3 * row_shift + col_shift], preferred_element_type...]
    unnamed x12 -> x15, local copies, waits for them, and re-layouts: 0.03 us -> 7.21 us
  transfers between devices with their start and end apart: 6 -> 0, of which waited for: 4 -> 0; matrix products, arithmetic and copies ran while one was open for 1% -> 0% of each run, Pallas kernels for 0% -> 0%
where the time goes in v1:
time: 70.3 us; the launch traced here: 70 us
  Pallas kernels  62.8 us (89%)
  local copies, waits for them, and re-layouts  7.21 us (10%)
    pallas_call x1, Pallas kernels, shards(): return call(video, gain1, sp1, tp1, gain2, sp2, tp2)  62.8 us
    unnamed x15, local copies, waits for them, and re-layouts  7.21 us

profile of v1, /device:TPU:25, one launch (start us, length us, event | category | flops | bytes accessed | tf_op | source)
XLA Modules:
  0.0 70.0 jit_solution(5308824950059318662)
XLA Ops:
  0.0 0.0 copy-start
  0.0 1.2 %copy-done = bf16[4,8,128,128]{3,2,1,0:T(8,128)(2,1)S(1)} copy-done((bf16[4,8,128,128]{3,2,1,0:T(8,128)(2,1)S(1)}, bf16[4,8,128,128]{3,2,1,0:T(8,128)(2,1)}, u32[]{:S(2)}) %copy-start) | copy-done | bytes 1048600
  1.2 0.0 copy-start.1
  1.2 1.0 %copy-done.1 = bf16[9,128,128]{2,1,0:T(8,128)(2,1)S(1)} copy-done((bf16[9,128,128]{2,1,0:T(8,128)(2,1)S(1)}, bf16[9,128,128]{2,1,0:T(8,128)(2,1)}, u32[]{:S(2)}) %copy-start.1) | copy-done | bytes 294936
  2.2 0.0 copy-start.2
  2.2 1.0 %copy-done.2 = bf16[9,128,128]{2,1,0:T(8,128)(2,1)S(1)} copy-done((bf16[9,128,128]{2,1,0:T(8,128)(2,1)S(1)}, bf16[9,128,128]{2,1,0:T(8,128)(2,1)}, u32[]{:S(2)}) %copy-start.2) | copy-done | bytes 294936
  3.1 0.0 copy-start.3
  3.2 0.9 %copy-done.3 = bf16[3,128,128]{2,1,0:T(8,128)(2,1)S(1)} copy-done((bf16[3,128,128]{2,1,0:T(8,128)(2,1)S(1)}, bf16[3,128,128]{2,1,0:T(8,128)(2,1)}, u32[]{:S(2)}) %copy-start.3) | copy-done | bytes 98328
  4.0 0.0 copy-start.4
  4.0 0.9 %copy-done.4 = bf16[3,128,128]{2,1,0:T(8,128)(2,1)S(1)} copy-done((bf16[3,128,128]{2,1,0:T(8,128)(2,1)S(1)}, bf16[3,128,128]{2,1,0:T(8,128)(2,1)}, u32[]{:S(2)}) %copy-start.4) | copy-done | bytes 98328
  4.9 0.0 copy-start.5
  4.9 0.7 copy-done.5
  5.6 0.0 copy-start.6
  5.6 0.7 copy-done.6
  6.2 62.8 %block.1 = bf16[4,8,128,128]{3,2,1,0:T(8,128)(2,1)S(1)} custom-call(bf16[4,8,128,128]{3,2,1,0:T(8,128)(2,1)S(1)} %copy-done, f32[128]{0:T(128)S(1)} %copy-done.5, bf16[9,128,128]{2,1,0:T(8,128)(2,1)S(1)} %copy-done.1, bf16[3,128,128]{2,1,0:T(8,128)(2,1)S(1)} %copy-done.3, f32[128]{0:T(128)S(1)} %copy-done.6, bf16[9,128,128]{2,1,0:T(8,128)(2,1)S(1)} %copy-done.2, ...), custom_call_target="tpu_custom_call" | custom-call | flops 4000000000 | bytes 4194304 | tf_op jit(solution)/shard_map/block/pallas_call | solution.py:406
  69.1 1.0 %copy.9 = bf16[4,8,128,128]{3,2,1,0:T(8,128)(2,1)} copy(bf16[4,8,128,128]{3,2,1,0:T(8,128)(2,1)S(1)} %block.1) | data formatting | bytes 2097152
Async XLA Ops:
  0.0 1.2 %copy-start = (bf16[4,8,128,128]{3,2,1,0:T(8,128)(2,1)S(1)}, bf16[4,8,128,128]{3,2,1,0:T(8,128)(2,1)}, u32[]{:S(2)}) copy-start(bf16[4,8,128,128]{3,2,1,0:T(8,128)(2,1)} %refs_0_.1) | copy-start | bytes 3145732
  1.2 1.0 %copy-start.1 = (bf16[9,128,128]{2,1,0:T(8,128)(2,1)S(1)}, bf16[9,128,128]{2,1,0:T(8,128)(2,1)}, u32[]{:S(2)}) copy-start(bf16[9,128,128]{2,1,0:T(8,128)(2,1)} %refs_2_.1) | copy-start | bytes 884740
  2.2 1.0 %copy-start.2 = (bf16[9,128,128]{2,1,0:T(8,128)(2,1)S(1)}, bf16[9,128,128]{2,1,0:T(8,128)(2,1)}, u32[]{:S(2)}) copy-start(bf16[9,128,128]{2,1,0:T(8,128)(2,1)} %refs_5_.1) | copy-start | bytes 884740
  3.1 0.9 %copy-start.3 = (bf16[3,128,128]{2,1,0:T(8,128)(2,1)S(1)}, bf16[3,128,128]{2,1,0:T(8,128)(2,1)}, u32[]{:S(2)}) copy-start(bf16[3,128,128]{2,1,0:T(8,128)(2,1)} %refs_3_.1) | copy-start | bytes 294916
  4.0 0.9 %copy-start.4 = (bf16[3,128,128]{2,1,0:T(8,128)(2,1)S(1)}, bf16[3,128,128]{2,1,0:T(8,128)(2,1)}, u32[]{:S(2)}) copy-start(bf16[3,128,128]{2,1,0:T(8,128)(2,1)} %refs_6_.1) | copy-start | bytes 294916
  4.9 0.7 copy-start.5
  5.6 0.7 copy-start.6

commit v2 on v1

v2 whole, which is shorter than its diff:
```python
import jax
import jax.numpy as jnp
from jax import lax
from jax.experimental import pallas as pl
from jax.experimental.pallas import tpu as pltpu
from jax.sharding import PartitionSpec as P

G = 32
C = 128
norm_eps = 1e-06

F32 = jnp.float32
BF16 = jnp.bfloat16

PARTS = 2


def kernel(
    members,
    video, gain1, sp1, tp1, gain2, sp2, tp2, out,
    xin, act, s1, s2, hid, w1, w2, t1, t2, g1, g2, st_send, st_recv, tot_send, tot_recv, relay,
    ld_sem, w_sem, st_ssem, st_rsem, h_ssem, h_rsem, y_ssem, y_rsem, rl_ssem, rl_rsem,
):
    frames, rows, cols, _ = video.shape
    pairs = rows // 2
    n_space, n_tm = lax.axis_size("space"), lax.axis_size("tm")
    space, tm = lax.axis_index("space"), lax.axis_index("tm")
    has_up, has_down = space > 0, space < n_space - 1
    has_before, has_after = tm > 0, tm < n_tm - 1
    cross = n_tm // 2 - 1
    crossing = tm == cross
    straight = jnp.logical_and(has_after, jnp.logical_not(crossing))
    relaying = tm == 0
    relayed = tm == cross + 1
    others = n_space - 1

    barrier = pltpu.get_barrier_semaphore()

    def greet(d, _):
        pl.semaphore_signal(barrier, 1, device_id={"space": lax.rem(space + d, n_space)})
        return 0

    lax.fori_loop(1, n_space, greet, 0)

    @pl.when(has_before)
    def _():
        pl.semaphore_signal(barrier, 1, device_id={"tm": tm - 1})

    @pl.when(has_after)
    def _():
        pl.semaphore_signal(barrier, 1, device_id={"tm": tm + 1})

    @pl.when(relaying)
    def _():
        pl.semaphore_signal(barrier, 1, device_id={"tm": cross})
        pl.semaphore_signal(barrier, 1, device_id={"tm": cross + 1})

    @pl.when(jnp.logical_or(crossing, relayed))
    def _():
        pl.semaphore_signal(barrier, 1, device_id={"tm": 0})

    loads = [
        pltpu.make_async_copy(video.at[f], xin.at[2 + f, pl.ds(1, rows)], ld_sem.at[f])
        for f in range(frames)
    ]
    for load in loads:
        load.start()
    weight_loads = [
        pltpu.make_async_copy(gain1, g1, w_sem.at[0]),
        pltpu.make_async_copy(sp1, w1.at[pl.ds(0, 9), :, pl.ds(0, C)], w_sem.at[1]),
        pltpu.make_async_copy(sp1, w1.at[pl.ds(3, 9), :, pl.ds(C, C)], w_sem.at[2]),
        pltpu.make_async_copy(tp1, t1.at[pl.ds(0, 3), :, pl.ds(0, C)], w_sem.at[3]),
        pltpu.make_async_copy(tp1, t1.at[pl.ds(1, 3), :, pl.ds(C, C)], w_sem.at[4]),
        pltpu.make_async_copy(gain2, g2, w_sem.at[5]),
        pltpu.make_async_copy(sp2, w2.at[pl.ds(0, 9), :, pl.ds(0, C)], w_sem.at[6]),
        pltpu.make_async_copy(sp2, w2.at[pl.ds(3, 9), :, pl.ds(C, C)], w_sem.at[7]),
        pltpu.make_async_copy(tp2, t2.at[pl.ds(0, 3), :, pl.ds(0, C)], w_sem.at[8]),
        pltpu.make_async_copy(tp2, t2.at[pl.ds(1, 3), :, pl.ds(C, C)], w_sem.at[9]),
    ]
    for load in weight_loads:
        load.start()
    for w in (w1, w2):
        w[pl.ds(9, 3), :, pl.ds(0, C)] = jnp.zeros((3, C, C), BF16)
        w[pl.ds(0, 3), :, pl.ds(C, C)] = jnp.zeros((3, C, C), BF16)
    for t in (t1, t2):
        t[pl.ds(3, 1), :, pl.ds(0, C)] = jnp.zeros((1, C, C), BF16)
        t[pl.ds(0, 1), :, pl.ds(C, C)] = jnp.zeros((1, C, C), BF16)

    def moments(x):
        x = x.reshape(-1, 8, C)
        return (
            jnp.sum(jnp.sum(x, axis=0), axis=0, keepdims=True),
            jnp.sum(jnp.sum(x * x, axis=0), axis=0, keepdims=True),
        )

    group = C // G
    lane = lax.broadcasted_iota(jnp.int32, (1, C), 1)

    def over_group(x):
        step = 1
        while step < group:
            low = lax.rem(lane, 2 * step) < step
            x = x + jnp.where(low, pltpu.roll(x, C - step, 1), pltpu.roll(x, step, 1))
            step *= 2
        return x

    def pack(rows_in):
        packed = jnp.zeros((1, C), F32)
        for i, x in enumerate(rows_in):
            packed = jnp.where(lax.rem(lane, group) == i, over_group(x), packed)
        return packed

    def unpack(packed, i):
        return over_group(jnp.where(lax.rem(lane, group) == i, packed, 0.0))

    def sizes(k):
        return 2 if k == 0 else 1

    def exchange(k, packed):
        n = sizes(k)
        for i, x in enumerate(packed):
            st_send[k, pl.ds(i, 1)] = x

        def send(d, _):
            pltpu.make_async_remote_copy(
                st_send.at[k, pl.ds(0, n)],
                st_recv.at[k, d - 1, pl.ds(0, n)],
                st_ssem.at[k],
                st_rsem.at[k],
                device_id={"space": lax.rem(space + d, n_space)},
            ).start()
            return 0

        lax.fori_loop(1, n_space, send, 0)

    def all_sums(k):
        n = sizes(k)
        whole = st_recv.at[k, pl.ds(0, others), pl.ds(0, n)]
        pltpu.make_async_copy(whole, whole, st_rsem.at[k]).wait()
        return [
            st_send[k, pl.ds(i, 1)] + jnp.sum(st_recv[k, :, pl.ds(i, 1)], axis=0) for i in range(n)
        ]

    def scales(total, square, gain):
        center = total / members
        inverse = lax.rsqrt(square / members - center * center + norm_eps)
        return center, inverse * gain * 0.5

    first_col = lax.broadcasted_iota(jnp.int32, (cols, C), 0) == 0
    last_col = lax.broadcasted_iota(jnp.int32, (cols, C), 0) == cols - 1

    def activate(src, f, q, center, half):
        h = (src[f, q].astype(F32) - center) * half
        a = h * (1.0 + jnp.tanh(h))
        left = jnp.where(first_col, 0.0, pltpu.roll(a, 1, 0))
        right = jnp.where(last_col, 0.0, pltpu.roll(a, cols - 1, 0))
        act[f, q // 2, q % 2, :, pl.ds(0, C)] = left.astype(BF16)
        act[f, q // 2, q % 2, :, pl.ds(C, C)] = a.astype(BF16)
        act[f, q // 2, q % 2, :, pl.ds(2 * C, C)] = right.astype(BF16)

    def activate_tile(src, f, center, half):
        def step(p, _):
            for o in (1, 2):
                activate(src, f, 2 * p + o, center, half)
            return 0

        lax.fori_loop(0, pairs, step, 0)

    def halo_copies(k, buf, e, n):
        up = pltpu.make_async_remote_copy(
            buf.at[pl.ds(e, n), 1],
            buf.at[pl.ds(e, n), rows + 1],
            h_ssem.at[k, 0],
            h_rsem.at[k, 0],
            device_id={"space": lax.max(space - 1, 0)},
        )
        down = pltpu.make_async_remote_copy(
            buf.at[pl.ds(e, n), rows],
            buf.at[pl.ds(e, n), 0],
            h_ssem.at[k, 1],
            h_rsem.at[k, 1],
            device_id={"space": lax.min(space + 1, n_space - 1)},
        )
        return up, down

    def send_halo(copies):
        up, down = copies

        @pl.when(has_up)
        def _():
            up.start()

        @pl.when(has_down)
        def _():
            down.start()

    def wait_halo_in(copies):
        up, down = copies

        @pl.when(has_down)
        def _():
            up.wait_recv()

        @pl.when(has_up)
        def _():
            down.wait_recv()

    def wait_halo_out(copies):
        up, down = copies

        @pl.when(has_up)
        def _():
            up.wait_send()

        @pl.when(has_down)
        def _():
            down.wait_send()

    def activate_halo(src, fs):
        for present, q in ((has_up, 0), (has_down, rows + 1)):

            @pl.when(present)
            def _():
                for f, center, half in fs:
                    activate(src, f, q, center, half)

            @pl.when(jnp.logical_not(present))
            def _():
                for f, _c, _h in fs:
                    act[f, q // 2, q % 2] = jnp.zeros((cols, 3 * C), BF16)

    np_ = pairs // PARTS

    def spatial(w, s, e, part):
        p0 = part * np_
        lhs = jnp.concatenate(
            [
                act[pl.ds(e, 2), pl.ds(p0 + i // 2, np_), i % 2].reshape(2 * np_ * cols, 3 * C)
                for i in range(4)
            ],
            axis=1,
        )
        o = jnp.dot(lhs, w[...].reshape(12 * C, 2 * C), preferred_element_type=F32)
        o = o.astype(BF16).reshape(2, np_, cols, 2 * C)
        s[pl.ds(e, 2), pl.ds(p0, np_), 0] = o[..., :C]
        s[pl.ds(e, 2), pl.ds(p0, np_), 1] = o[..., C:]

    def temporal(t, s, e, part):
        p0 = part * np_
        lhs = jnp.concatenate(
            [s[e - 2 + i, pl.ds(p0, np_)].reshape(2 * np_ * cols, C) for i in range(4)], axis=1
        )
        return jnp.dot(lhs, t[...].reshape(4 * C, 2 * C), preferred_element_type=F32)

    mid = rows // 2
    pieces = [(1, 1), (rows, 1), (2, mid - 1), (mid + 1, mid - 1)]
    last = len(pieces) - 1
    total_at = len(pieces)

    def onward(k, buf, piece):
        r, n = pieces[piece]
        return pltpu.make_async_remote_copy(
            buf.at[pl.ds(frames, 2), pl.ds(r, n)],
            buf.at[pl.ds(0, 2), pl.ds(r, n)],
            y_ssem.at[k, piece],
            y_rsem.at[k, piece],
            device_id={"tm": lax.min(tm + 1, n_tm - 1)},
        )

    def onward_total(k):
        return pltpu.make_async_remote_copy(
            tot_send.at[k],
            tot_recv.at[k],
            y_ssem.at[k, total_at],
            y_rsem.at[k, total_at],
            device_id={"tm": lax.min(tm + 1, n_tm - 1)},
        )

    def to_relay(k, buf):
        r, n = pieces[last]
        return pltpu.make_async_remote_copy(
            buf.at[pl.ds(frames, 2), pl.ds(r, n)],
            relay.at[k],
            y_ssem.at[k, last],
            rl_rsem.at[k],
            device_id={"tm": 0},
        )

    def from_relay(k, buf):
        r, n = pieces[last]
        return pltpu.make_async_remote_copy(
            relay.at[k],
            buf.at[pl.ds(0, 2), pl.ds(r, n)],
            rl_ssem.at[k],
            y_rsem.at[k, last],
            device_id={"tm": cross + 1},
        )

    def send_total(k, packed):
        tot_send[k] = packed

        @pl.when(has_after)
        def _():
            onward_total(k).start()

    def pass_edges(k, buf, copies):
        @pl.when(has_before)
        def _():
            onward(k, buf, 0).wait_recv()
            onward(k, buf, 1).wait_recv()
            send_halo(copies)

    def pass_relay(k, buf):
        @pl.when(relaying)
        def _():
            to_relay(k, buf).wait_recv()
            from_relay(k, buf).start()

    def earlier_scales(k, gain):
        onward_total(k).wait_recv()
        packed = tot_recv[k]
        return pair_scales(packed, gain)

    def pair_scales(packed, gain):
        return [scales(unpack(packed, j), unpack(packed, 2 + j), gain) for j in range(2)]

    def activate_pair(src, e, pair, copies):
        fs = [(e + j, *pair[j]) for j in range(2)]
        for f in fs:
            activate_tile(src, *f)
        if copies is not None:
            wait_halo_in(copies)
        activate_halo(src, fs)

    def earlier(k, buf, w, s, gain, copies):
        @pl.when(has_before)
        def _():
            pair = earlier_scales(k, gain)
            for piece in (2, 3):
                onward(k, buf, piece).wait_recv()
            activate_pair(buf, 0, pair, copies)
            for part in range(PARTS):
                spatial(w, s, 0, part)

        @pl.when(jnp.logical_not(has_before))
        def _():
            s[0] = s[2]
            s[1] = s[2]

    def hidden_part(e, part):
        h = temporal(t1, s1, e, part).astype(BF16)
        own = pl.ds(1 + part * 2 * np_, 2 * np_)
        sums = []
        for j in range(2):
            hj = h[:, j * C : (j + 1) * C]
            hid[e + j, own] = hj.reshape(2 * np_, cols, C)
            sums.append(moments(hj.astype(F32)))
        return [sums[0][0], sums[1][0], sums[0][1], sums[1][1]]

    def hidden(k, e):
        sums = None
        for part in range(PARTS):
            new = hidden_part(e, part)
            sums = new if sums is None else [a + b for a, b in zip(sums, new)]
        exchange(k, [pack(sums)])

    def finish(f0, part):
        r = temporal(t2, s2, 2 + f0, part)
        rows_here = 2 * np_
        r0 = part * rows_here
        for j in range(2):
            v = xin[2 + f0 + j, pl.ds(1 + r0, rows_here)].astype(F32)
            total = v + r[:, j * C : (j + 1) * C].reshape(rows_here, cols, C)
            out[f0 + j, pl.ds(r0, rows_here)] = total.astype(BF16)

    sums = []
    for f in range(frames):
        loads[f].wait()

        def add(p, c, f=f):
            x = xin[2 + f, pl.ds(1 + 2 * p, 2)].astype(F32).reshape(-1, 8, C)
            return c[0] + jnp.sum(x, axis=0), c[1] + jnp.sum(x * x, axis=0)

        zero = jnp.zeros((8, C), F32)
        a, b = lax.fori_loop(0, pairs, add, (zero, zero))
        sums.append((jnp.sum(a, axis=0, keepdims=True), jnp.sum(b, axis=0, keepdims=True)))
    packed = [
        pack([sums[f][0], sums[f + 1][0], sums[f][1], sums[f + 1][1]]) for f in range(0, frames, 2)
    ]

    greeted = others + has_before.astype(jnp.int32) + has_after.astype(jnp.int32)
    greeted = greeted + 2 * relaying.astype(jnp.int32)
    greeted = greeted + crossing.astype(jnp.int32) + relayed.astype(jnp.int32)
    pl.semaphore_wait(barrier, greeted)
    exchange(0, packed)
    halo0 = halo_copies(0, xin, 2, frames)
    halo1 = halo_copies(1, hid, 4, 2)
    halo2 = halo_copies(2, hid, 2, 2)
    halo3 = halo_copies(3, xin, 0, 2)
    halo4 = halo_copies(4, hid, 0, 2)

    @pl.when(straight)
    def _():
        for piece in range(len(pieces)):
            onward(0, xin, piece).start()

    @pl.when(crossing)
    def _():
        to_relay(0, xin).start()
        onward(0, xin, 0).start()
        onward(0, xin, 1).start()

    send_halo(halo0)

    @pl.when(crossing)
    def _():
        onward(0, xin, 2).start()

    for load in weight_loads:
        load.wait()
    gain_first = g1[...].reshape(1, C)
    gain_second = g2[...].reshape(1, C)
    pass_relay(0, xin)
    pass_edges(0, xin, halo3)
    whole01, whole23 = all_sums(0)
    send_total(0, whole23)
    pair01, pair23 = pair_scales(whole01, gain_first), pair_scales(whole23, gain_first)

    activate_pair(xin, 4, pair23, halo0)
    for part in range(PARTS):
        spatial(w1, s1, 4, part)
    activate_pair(xin, 2, pair01, None)
    for part in range(PARTS):
        spatial(w1, s1, 2, part)
    hidden(1, 4)

    @pl.when(straight)
    def _():
        for piece in range(len(pieces) - 1):
            onward(1, hid, piece).start()

    @pl.when(crossing)
    def _():
        to_relay(1, hid).start()
        onward(1, hid, 0).start()
        onward(1, hid, 1).start()

    send_halo(halo1)

    @pl.when(crossing)
    def _():
        onward(1, hid, 2).start()

    earlier(0, xin, w1, s1, gain_first, halo3)
    hidden(2, 2)
    send_halo(halo2)

    (whole23,) = all_sums(1)
    send_total(1, whole23)

    @pl.when(straight)
    def _():
        onward(1, hid, last).start()

    activate_pair(hid, 4, pair_scales(whole23, gain_second), halo1)
    for part in range(PARTS):
        spatial(w2, s2, 4, part)
    pass_relay(1, hid)
    pass_edges(1, hid, halo4)

    (whole01,) = all_sums(2)
    activate_pair(hid, 2, pair_scales(whole01, gain_second), halo2)
    for part in range(PARTS):
        spatial(w2, s2, 2, part)
    for part in range(PARTS):
        finish(2, part)
    earlier(1, hid, w2, s2, gain_second, halo4)
    for part in range(PARTS):
        finish(0, part)

    for copies in (halo0, halo1, halo2):
        wait_halo_out(copies)
    for k in range(3):
        whole = st_recv.at[k, pl.ds(0, others), pl.ds(0, sizes(k))]
        pltpu.make_async_copy(whole, whole, st_ssem.at[k]).wait()

    @pl.when(has_before)
    def _():
        for copies in (halo3, halo4):
            wait_halo_out(copies)

    @pl.when(has_after)
    def _():
        for k, buf in ((0, xin), (1, hid)):
            for piece in range(len(pieces)):
                onward(k, buf, piece).wait_send()
            onward_total(k).wait_send()

    @pl.when(relaying)
    def _():
        for k, buf in ((0, xin), (1, hid)):
            from_relay(k, buf).wait_send()


def shards(video, gain1, sp1, tp1, gain2, sp2, tp2):
    frames, rows, cols, channels = video.shape
    n_space = lax.axis_size("space")
    members = rows * n_space * cols * (channels // G)
    hbm = pl.BlockSpec(memory_space=pltpu.HBM)
    inputs = (video, gain1, sp1, tp1, gain2, sp2, tp2)
    call = pl.pallas_call(
        lambda *refs: kernel(float(members), *refs),
        out_shape=pltpu.VMEM(video.shape, BF16),
        in_specs=[hbm] * 7,
        out_specs=pl.BlockSpec(memory_space=pltpu.VMEM),
        scratch_shapes=[
            pltpu.VMEM((frames + 2, rows + 2, cols, C), BF16),
            pltpu.VMEM((frames + 2, rows // 2 + 1, 2, cols, 3 * C), BF16),
            pltpu.VMEM((frames + 2, rows // 2, 2, cols, C), BF16),
            pltpu.VMEM((frames + 2, rows // 2, 2, cols, C), BF16),
            pltpu.VMEM((frames + 2, rows + 2, cols, C), BF16),
            pltpu.VMEM((12, C, 2 * C), BF16),
            pltpu.VMEM((12, C, 2 * C), BF16),
            pltpu.VMEM((4, C, 2 * C), BF16),
            pltpu.VMEM((4, C, 2 * C), BF16),
            pltpu.VMEM((C,), F32),
            pltpu.VMEM((C,), F32),
            pltpu.VMEM((3, 8, C), F32),
            pltpu.VMEM((3, n_space - 1, 8, C), F32),
            pltpu.VMEM((2, 1, C), F32),
            pltpu.VMEM((2, 1, C), F32),
            pltpu.VMEM((2, 2, rows // 2 - 1, cols, C), BF16),
            pltpu.SemaphoreType.DMA((frames,)),
            pltpu.SemaphoreType.DMA((10,)),
            pltpu.SemaphoreType.DMA((3,)),
            pltpu.SemaphoreType.DMA((3,)),
            pltpu.SemaphoreType.DMA((5, 2)),
            pltpu.SemaphoreType.DMA((5, 2)),
            pltpu.SemaphoreType.DMA((2, 5)),
            pltpu.SemaphoreType.DMA((2, 5)),
            pltpu.SemaphoreType.DMA((2,)),
            pltpu.SemaphoreType.DMA((2,)),
        ],
        compiler_params=pltpu.CompilerParams(
            collective_id=0, has_side_effects=True, vmem_limit_bytes=62 * 2**20
        ),
        cost_estimate=pl.CostEstimate(
            flops=4 * 10**9, bytes_accessed=4 * 2**20, transcendentals=10**6
        ),
        name="block",
    )
    return call(*[pltpu.with_memory_space_constraint(x, pltpu.HBM) for x in inputs])


def solution(mesh):
    in_specs = (P("tm", "space", None, None), P(), P(), P(), P(), P(), P())
    out_specs = P("tm", "space", None, None)
    return jax.shard_map(shards, mesh=mesh, in_specs=in_specs, out_specs=out_specs, check_vma=False)
```

time: 70.3 us -> 42.9 us (0.61)
  Pallas kernels: 62.8 us -> 41.8 us
  local copies, waits for them, and re-layouts: 7.21 us -> 0.97 us
    pallas_call x1, Pallas kernels: 62.8 us -> 41.8 us  [shards(): call(*[pltpu.with_memory_space_constraint(x, pltpu.HBM) for x in inputs])]
    unnamed x15 -> x1, local copies, waits for them, and re-layouts: 7.21 us -> 0.97 us
where the time goes in v2:
time: 42.9 us; the launch traced here: 42.8 us
  Pallas kernels  41.8 us (97%)
  local copies, waits for them, and re-layouts  0.97 us (2%)
    pallas_call x1, Pallas kernels, shards(): call(*[pltpu.with_memory_space_constraint(x, pltpu.HBM) for x in inputs])  41.8 us
    unnamed x1, local copies, waits for them, and re-layouts  0.97 us

profile of v2, /device:TPU:25, one launch (start us, length us, event | category | flops | bytes accessed | tf_op | source)
XLA Modules:
  0.0 42.8 jit_solution(5536058351993166913)
XLA Ops:
  0.0 41.8 %block.1 = bf16[4,8,128,128]{3,2,1,0:T(8,128)(2,1)S(1)} custom-call(bf16[4,8,128,128]{3,2,1,0:T(8,128)(2,1)} %refs_0_.1, f32[128]{0:T(128)} %refs_1_.1, bf16[9,128,128]{2,1,0:T(8,128)(2,1)} %refs_2_.1, bf16[3,128,128]{2,1,0:T(8,128)(2,1)} %refs_3_.1, f32[128]{0:T(128)} %refs_4_.1, bf16[9,128,128]{2,1,0:T(8,128)(2,1)} %refs_5_.1, bf16[3,128,128]{2,1,0:T(8,128)(2,1)} %refs_6_.1), custom_call_target="tpu_custom_call" | custom-call | flops 4000000000 | bytes 4194304 | tf_op jit(solution)/shard_map/block/pallas_call | solution.py:552
  41.8 1.0 %copy.9 = bf16[4,8,128,128]{3,2,1,0:T(8,128)(2,1)} copy(bf16[4,8,128,128]{3,2,1,0:T(8,128)(2,1)S(1)} %block.1) | data formatting | bytes 2097152

commit v3 on v2

--- a/solution.py
+++ b/solution.py
@@ -13,6 +13,17 @@
 BF16 = jnp.bfloat16
 
 PARTS = 2
+
+
+def steps(n_space):
+    n_x = n_space // 8
+
+    def hops(step):
+        x, z, core = step
+        return min(x, n_x - x) + 2 * min(z, 4 - z) + core / 4
+
+    every = [(x, z, core) for x in range(n_x) for z in range(4) for core in range(2)]
+    return sorted((s for s in every if s != (0, 0, 0)), key=hops, reverse=True)
 
 
 def kernel(
@@ -33,14 +44,18 @@
     relaying = tm == 0
     relayed = tm == cross + 1
     others = n_space - 1
+    apart = steps(n_space)
+
+    def tile(place):
+        x, z, core = apart[place]
+        across = lax.rem(space // 8 + x, n_space // 8)
+        along = lax.rem(lax.rem(space // 2, 4) + z, 4)
+        return across * 8 + along * 2 + lax.rem(space + core, 2)
 
     barrier = pltpu.get_barrier_semaphore()
 
-    def greet(d, _):
-        pl.semaphore_signal(barrier, 1, device_id={"space": lax.rem(space + d, n_space)})
-        return 0
-
-    lax.fori_loop(1, n_space, greet, 0)
+    for place in range(others):
+        pl.semaphore_signal(barrier, 1, device_id={"space": tile(place)})
 
     @pl.when(has_before)
     def _():
@@ -121,17 +136,14 @@
         for i, x in enumerate(packed):
             st_send[k, pl.ds(i, 1)] = x
 
-        def send(d, _):
+        for place in range(others):
             pltpu.make_async_remote_copy(
                 st_send.at[k, pl.ds(0, n)],
-                st_recv.at[k, d - 1, pl.ds(0, n)],
+                st_recv.at[k, place, pl.ds(0, n)],
                 st_ssem.at[k],
                 st_rsem.at[k],
-                device_id={"space": lax.rem(space + d, n_space)},
+                device_id={"space": tile(place)},
             ).start()
-            return 0
-
-        lax.fori_loop(1, n_space, send, 0)
 
     def all_sums(k):
         n = sizes(k)
@@ -253,8 +265,9 @@
         return jnp.dot(lhs, t[...].reshape(4 * C, 2 * C), preferred_element_type=F32)
 
     mid = rows // 2
-    pieces = [(1, 1), (rows, 1), (2, mid - 1), (mid + 1, mid - 1)]
-    last = len(pieces) - 1
+    pieces = [(1, 1), (rows, 1), (2, 1), (3, mid - 2), (mid + 1, 1), (mid + 2, mid - 2)]
+    held = 4
+    detour = (3, 4, 5)
     total_at = len(pieces)
 
     def onward(k, buf, piece):
@@ -276,32 +289,60 @@
             device_id={"tm": lax.min(tm + 1, n_tm - 1)},
         )
 
-    def to_relay(k, buf):
-        r, n = pieces[last]
+    def at_relay(k, piece):
+        r, n = pieces[piece]
+        return relay.at[k, :, pl.ds(r, n)]
+
+    def to_relay(k, buf, piece):
+        r, n = pieces[piece]
         return pltpu.make_async_remote_copy(
             buf.at[pl.ds(frames, 2), pl.ds(r, n)],
-            relay.at[k],
-            y_ssem.at[k, last],
-            rl_rsem.at[k],
+            at_relay(k, piece),
+            y_ssem.at[k, piece],
+            rl_rsem.at[k, piece],
             device_id={"tm": 0},
         )
 
-    def from_relay(k, buf):
-        r, n = pieces[last]
+    def from_relay(k, buf, piece):
+        r, n = pieces[piece]
         return pltpu.make_async_remote_copy(
-            relay.at[k],
+            at_relay(k, piece),
             buf.at[pl.ds(0, 2), pl.ds(r, n)],
-            rl_ssem.at[k],
-            y_rsem.at[k, last],
+            rl_ssem.at[k, piece],
+            y_rsem.at[k, piece],
             device_id={"tm": cross + 1},
         )
 
-    def send_total(k, packed):
+    def send_first(k, buf):
+        @pl.when(straight)
+        def _():
+            for piece in range(held):
+                onward(k, buf, piece).start()
+
+        @pl.when(crossing)
+        def _():
+            for piece in detour:
+                to_relay(k, buf, piece).start()
+
+    def send_cross(k, buf, some):
+        @pl.when(crossing)
+        def _():
+            for piece in some:
+                if piece not in detour:
+                    onward(k, buf, piece).start()
+
+    def send_rest(k, buf, packed):
         tot_send[k] = packed
 
         @pl.when(has_after)
         def _():
             onward_total(k).start()
+
+        @pl.when(straight)
+        def _():
+            for piece in range(held, len(pieces)):
+                onward(k, buf, piece).start()
+
 
     def pass_edges(k, buf, copies):
         @pl.when(has_before)
@@ -310,11 +351,12 @@
             onward(k, buf, 1).wait_recv()
             send_halo(copies)
 
-    def pass_relay(k, buf):
+    def pass_relay(k, buf, pieces):
         @pl.when(relaying)
         def _():
-            to_relay(k, buf).wait_recv()
-            from_relay(k, buf).start()
+            for piece in pieces:
+                to_relay(k, buf, piece).wait_recv()
+                from_relay(k, buf, piece).start()
 
     def earlier_scales(k, gain):
         onward_total(k).wait_recv()
@@ -332,20 +374,43 @@
             wait_halo_in(copies)
         activate_halo(src, fs)
 
-    def earlier(k, buf, w, s, gain, copies):
+    def activate_rows(src, fs, r, n):
+        def step(q, _):
+            for f in fs:
+                activate(src, f[0], q, f[1], f[2])
+            return 0
+
+        lax.fori_loop(r, r + n, step, 0)
+
+    def earlier(k, buf, w, s, gain, copies, then):
         @pl.when(has_before)
         def _():
-            pair = earlier_scales(k, gain)
-            for piece in (2, 3):
-                onward(k, buf, piece).wait_recv()
-            activate_pair(buf, 0, pair, copies)
-            for part in range(PARTS):
-                spatial(w, s, 0, part)
+            fs = [(j, *pair) for j, pair in enumerate(earlier_scales(k, gain))]
+            onward(k, buf, 2).wait_recv()
+            onward(k, buf, 3).wait_recv()
+            activate_rows(buf, fs, 1, mid)
+            activate_rows(buf, fs, rows, 1)
+            wait_halo_in(copies)
+            activate_halo(buf, fs)
+            onward(k, buf, 4).wait_recv()
+            activate_rows(buf, fs, mid + 1, 1)
+            spatial(w, s, 0, 0)
 
         @pl.when(jnp.logical_not(has_before))
         def _():
             s[0] = s[2]
             s[1] = s[2]
+
+        then(0)
+
+        @pl.when(has_before)
+        def _():
+            fs = [(j, *pair) for j, pair in enumerate(pair_scales(tot_recv[k], gain))]
+            onward(k, buf, 5).wait_recv()
+            activate_rows(buf, fs, mid + 2, mid - 2)
+            spatial(w, s, 0, 1)
+
+        then(1)
 
     def hidden_part(e, part):
         h = temporal(t1, s1, e, part).astype(BF16)
@@ -357,11 +422,8 @@
             sums.append(moments(hj.astype(F32)))
         return [sums[0][0], sums[1][0], sums[0][1], sums[1][1]]
 
-    def hidden(k, e):
-        sums = None
-        for part in range(PARTS):
-            new = hidden_part(e, part)
-            sums = new if sums is None else [a + b for a, b in zip(sums, new)]
+    def hidden(k, e, parts):
+        sums = [a + b for a, b in zip(*parts)]
         exchange(k, [pack(sums)])
 
     def finish(f0, part):
@@ -390,83 +452,57 @@
 
     greeted = others + has_before.astype(jnp.int32) + has_after.astype(jnp.int32)
     greeted = greeted + 2 * relaying.astype(jnp.int32)
-    greeted = greeted + crossing.astype(jnp.int32) + relayed.astype(jnp.int32)
+    greeted = greeted + jnp.logical_or(crossing, relayed).astype(jnp.int32)
     pl.semaphore_wait(barrier, greeted)
+    send_first(0, xin)
     exchange(0, packed)
     halo0 = halo_copies(0, xin, 2, frames)
     halo1 = halo_copies(1, hid, 4, 2)
     halo2 = halo_copies(2, hid, 2, 2)
     halo3 = halo_copies(3, xin, 0, 2)
     halo4 = halo_copies(4, hid, 0, 2)
-
-    @pl.when(straight)
-    def _():
-        for piece in range(len(pieces)):
-            onward(0, xin, piece).start()
-
-    @pl.when(crossing)
-    def _():
-        to_relay(0, xin).start()
-        onward(0, xin, 0).start()
-        onward(0, xin, 1).start()
-
+    send_cross(0, xin, (0, 1))
     send_halo(halo0)
-
-    @pl.when(crossing)
-    def _():
-        onward(0, xin, 2).start()
+    send_cross(0, xin, (2,))
 
     for load in weight_loads:
         load.wait()
     gain_first = g1[...].reshape(1, C)
     gain_second = g2[...].reshape(1, C)
-    pass_relay(0, xin)
     pass_edges(0, xin, halo3)
+    pass_relay(0, xin, (3,))
     whole01, whole23 = all_sums(0)
-    send_total(0, whole23)
+    send_rest(0, xin, whole23)
+    pass_relay(0, xin, (4,))
     pair01, pair23 = pair_scales(whole01, gain_first), pair_scales(whole23, gain_first)
 
     activate_pair(xin, 4, pair23, halo0)
     for part in range(PARTS):
         spatial(w1, s1, 4, part)
+    pass_relay(0, xin, (5,))
     activate_pair(xin, 2, pair01, None)
     for part in range(PARTS):
         spatial(w1, s1, 2, part)
-    hidden(1, 4)
-
-    @pl.when(straight)
-    def _():
-        for piece in range(len(pieces) - 1):
-            onward(1, hid, piece).start()
-
-    @pl.when(crossing)
-    def _():
-        to_relay(1, hid).start()
-        onward(1, hid, 0).start()
-        onward(1, hid, 1).start()
-
+    hidden(1, 4, [hidden_part(4, part) for part in range(PARTS)])
+    send_first(1, hid)
+    send_cross(1, hid, (0, 1))
     send_halo(halo1)
 
-    @pl.when(crossing)
-    def _():
-        onward(1, hid, 2).start()
-
-    earlier(0, xin, w1, s1, gain_first, halo3)
-    hidden(2, 2)
+    parts = []
+    earlier(0, xin, w1, s1, gain_first, halo3, lambda part: parts.append(hidden_part(2, part)))
+    hidden(2, 2, parts)
     send_halo(halo2)
-
+    send_cross(1, hid, (2,))
+
+    pass_edges(1, hid, halo4)
+    pass_relay(1, hid, (3,))
     (whole23,) = all_sums(1)
-    send_total(1, whole23)
-
-    @pl.when(straight)
-    def _():
-        onward(1, hid, last).start()
-
+    send_rest(1, hid, whole23)
+    pass_relay(1, hid, (4,))
     activate_pair(hid, 4, pair_scales(whole23, gain_second), halo1)
     for part in range(PARTS):
         spatial(w2, s2, 4, part)
-    pass_relay(1, hid)
-    pass_edges(1, hid, halo4)
+    pass_relay(1, hid, (5,))
 
     (whole01,) = all_sums(2)
     activate_pair(hid, 2, pair_scales(whole01, gain_second), halo2)
@@ -474,9 +510,7 @@
         spatial(w2, s2, 2, part)
     for part in range(PARTS):
         finish(2, part)
-    earlier(1, hid, w2, s2, gain_second, halo4)
-    for part in range(PARTS):
-        finish(0, part)
+    earlier(1, hid, w2, s2, gain_second, halo4, lambda part: finish(0, part))
 
     for copies in (halo0, halo1, halo2):
         wait_halo_out(copies)
@@ -496,10 +530,12 @@
                 onward(k, buf, piece).wait_send()
             onward_total(k).wait_send()
 
-    @pl.when(relaying)
-    def _():
-        for k, buf in ((0, xin), (1, hid)):
-            from_relay(k, buf).wait_send()
+    for k, buf in ((0, xin), (1, hid)):
+
+        @pl.when(relaying)
+        def _():
+            for piece in detour:
+                from_relay(k, buf, piece).wait_send()
 
 
 def shards(video, gain1, sp1, tp1, gain2, sp2, tp2):
@@ -529,17 +565,17 @@
             pltpu.VMEM((3, n_space - 1, 8, C), F32),
             pltpu.VMEM((2, 1, C), F32),
             pltpu.VMEM((2, 1, C), F32),
-            pltpu.VMEM((2, 2, rows // 2 - 1, cols, C), BF16),
+            pltpu.VMEM((2, 2, rows + 2, cols, C), BF16),
             pltpu.SemaphoreType.DMA((frames,)),
             pltpu.SemaphoreType.DMA((10,)),
             pltpu.SemaphoreType.DMA((3,)),
             pltpu.SemaphoreType.DMA((3,)),
             pltpu.SemaphoreType.DMA((5, 2)),
             pltpu.SemaphoreType.DMA((5, 2)),
-            pltpu.SemaphoreType.DMA((2, 5)),
-            pltpu.SemaphoreType.DMA((2, 5)),
-            pltpu.SemaphoreType.DMA((2,)),
-            pltpu.SemaphoreType.DMA((2,)),
+            pltpu.SemaphoreType.DMA((2, 7)),
+            pltpu.SemaphoreType.DMA((2, 7)),
+            pltpu.SemaphoreType.DMA((2, 7)),
+            pltpu.SemaphoreType.DMA((2, 7)),
         ],
         compiler_params=pltpu.CompilerParams(
             collective_id=0, has_side_effects=True, vmem_limit_bytes=62 * 2**20

time: 42.9 us -> 40.1 us (0.935)
  Pallas kernels: 41.8 us -> 39 us
    pallas_call x1, Pallas kernels: 41.8 us -> 39 us  [shards(): call(*[pltpu.with_memory_space_constraint(x, pltpu.HBM) for x in inputs])]
where the time goes in v3:
time: 40.1 us; the launch traced here: 40 us
  Pallas kernels  39 us (97%)
  local copies, waits for them, and re-layouts  0.97 us (2%)
    pallas_call x1, Pallas kernels, shards(): call(*[pltpu.with_memory_space_constraint(x, pltpu.HBM) for x in inputs])  39 us
    unnamed x1, local copies, waits for them, and re-layouts  0.97 us

profile of v3, /device:TPU:25, one launch (start us, length us, event | category | flops | bytes accessed | tf_op | source)
XLA Modules:
  0.0 40.0 jit_solution(11663803732718140303)
XLA Ops:
  0.0 39.0 %block.1 = bf16[4,8,128,128]{3,2,1,0:T(8,128)(2,1)S(1)} custom-call(bf16[4,8,128,128]{3,2,1,0:T(8,128)(2,1)} %refs_0_.1, f32[128]{0:T(128)} %refs_1_.1, bf16[9,128,128]{2,1,0:T(8,128)(2,1)} %refs_2_.1, bf16[3,128,128]{2,1,0:T(8,128)(2,1)} %refs_3_.1, f32[128]{0:T(128)} %refs_4_.1, bf16[9,128,128]{2,1,0:T(8,128)(2,1)} %refs_5_.1, bf16[3,128,128]{2,1,0:T(8,128)(2,1)} %refs_6_.1), custom_call_target="tpu_custom_call" | custom-call | flops 4000000000 | bytes 4194304 | tf_op jit(solution)/shard_map/block/pallas_call | solution.py:588
  39.0 1.0 %copy.9 = bf16[4,8,128,128]{3,2,1,0:T(8,128)(2,1)} copy(bf16[4,8,128,128]{3,2,1,0:T(8,128)(2,1)S(1)} %block.1) | data formatting | bytes 2097152

commit v4 on v3

--- a/solution.py
+++ b/solution.py
@@ -344,8 +344,10 @@
                 onward(k, buf, piece).start()
 
 
-    def pass_edges(k, buf, copies):
-        @pl.when(has_before)
+    unrelayed = jnp.logical_and(has_before, jnp.logical_not(relayed))
+
+    def pass_edges(k, buf, copies, when):
+        @pl.when(when)
         def _():
             onward(k, buf, 0).wait_recv()
             onward(k, buf, 1).wait_recv()
@@ -370,8 +372,7 @@
         fs = [(e + j, *pair[j]) for j in range(2)]
         for f in fs:
             activate_tile(src, *f)
-        if copies is not None:
-            wait_halo_in(copies)
+        wait_halo_in(copies)
         activate_halo(src, fs)
 
     def activate_rows(src, fs, r, n):
@@ -456,20 +457,21 @@
     pl.semaphore_wait(barrier, greeted)
     send_first(0, xin)
     exchange(0, packed)
-    halo0 = halo_copies(0, xin, 2, frames)
+    halo0 = halo_copies(0, xin, 4, 2)
+    halo5 = halo_copies(5, xin, 2, 2)
     halo1 = halo_copies(1, hid, 4, 2)
     halo2 = halo_copies(2, hid, 2, 2)
     halo3 = halo_copies(3, xin, 0, 2)
     halo4 = halo_copies(4, hid, 0, 2)
-    send_cross(0, xin, (0, 1))
     send_halo(halo0)
-    send_cross(0, xin, (2,))
+    send_halo(halo5)
+    send_cross(0, xin, (0, 1, 2))
 
     for load in weight_loads:
         load.wait()
     gain_first = g1[...].reshape(1, C)
     gain_second = g2[...].reshape(1, C)
-    pass_edges(0, xin, halo3)
+    pass_edges(0, xin, halo3, unrelayed)
     pass_relay(0, xin, (3,))
     whole01, whole23 = all_sums(0)
     send_rest(0, xin, whole23)
@@ -480,29 +482,31 @@
     for part in range(PARTS):
         spatial(w1, s1, 4, part)
     pass_relay(0, xin, (5,))
-    activate_pair(xin, 2, pair01, None)
+    pass_edges(0, xin, halo3, relayed)
+    activate_pair(xin, 2, pair01, halo5)
     for part in range(PARTS):
         spatial(w1, s1, 2, part)
     hidden(1, 4, [hidden_part(4, part) for part in range(PARTS)])
     send_first(1, hid)
+    send_halo(halo1)
     send_cross(1, hid, (0, 1))
-    send_halo(halo1)
 
     parts = []
     earlier(0, xin, w1, s1, gain_first, halo3, lambda part: parts.append(hidden_part(2, part)))
     hidden(2, 2, parts)
     send_halo(halo2)
-    send_cross(1, hid, (2,))
-
-    pass_edges(1, hid, halo4)
+
+    pass_edges(1, hid, halo4, unrelayed)
     pass_relay(1, hid, (3,))
     (whole23,) = all_sums(1)
     send_rest(1, hid, whole23)
+    send_cross(1, hid, (2,))
     pass_relay(1, hid, (4,))
     activate_pair(hid, 4, pair_scales(whole23, gain_second), halo1)
     for part in range(PARTS):
         spatial(w2, s2, 4, part)
     pass_relay(1, hid, (5,))
+    pass_edges(1, hid, halo4, relayed)
 
     (whole01,) = all_sums(2)
     activate_pair(hid, 2, pair_scales(whole01, gain_second), halo2)
@@ -512,7 +516,7 @@
         finish(2, part)
     earlier(1, hid, w2, s2, gain_second, halo4, lambda part: finish(0, part))
 
-    for copies in (halo0, halo1, halo2):
+    for copies in (halo0, halo1, halo2, halo5):
         wait_halo_out(copies)
     for k in range(3):
         whole = st_recv.at[k, pl.ds(0, others), pl.ds(0, sizes(k))]
@@ -570,8 +574,8 @@
             pltpu.SemaphoreType.DMA((10,)),
             pltpu.SemaphoreType.DMA((3,)),
             pltpu.SemaphoreType.DMA((3,)),
-            pltpu.SemaphoreType.DMA((5, 2)),
-            pltpu.SemaphoreType.DMA((5, 2)),
+            pltpu.SemaphoreType.DMA((6, 2)),
+            pltpu.SemaphoreType.DMA((6, 2)),
             pltpu.SemaphoreType.DMA((2, 7)),
             pltpu.SemaphoreType.DMA((2, 7)),
             pltpu.SemaphoreType.DMA((2, 7)),

time: 40.1 us -> 38.9 us (0.970)
  the two profiles are of different devices: /device:TPU:25 before, /device:TPU:32 now
where the time goes in v4:
time: 38.9 us; the launch traced here: 38.8 us
  Pallas kernels  37.8 us (97%)
  local copies, waits for them, and re-layouts  0.97 us (2%)
    pallas_call x1, Pallas kernels, shards(): call(*[pltpu.with_memory_space_constraint(x, pltpu.HBM) for x in inputs])  37.8 us
    unnamed x1, local copies, waits for them, and re-layouts  0.97 us

profile of v4, /device:TPU:32, one launch (start us, length us, event | category | flops | bytes accessed | tf_op | source)
XLA Modules:
  0.0 38.8 jit_solution(16187185724730163639)
XLA Ops:
  0.0 37.8 %block.1 = bf16[4,8,128,128]{3,2,1,0:T(8,128)(2,1)S(1)} custom-call(bf16[4,8,128,128]{3,2,1,0:T(8,128)(2,1)} %refs_0_.1, f32[128]{0:T(128)} %refs_1_.1, bf16[9,128,128]{2,1,0:T(8,128)(2,1)} %refs_2_.1, bf16[3,128,128]{2,1,0:T(8,128)(2,1)} %refs_3_.1, f32[128]{0:T(128)} %refs_4_.1, bf16[9,128,128]{2,1,0:T(8,128)(2,1)} %refs_5_.1, bf16[3,128,128]{2,1,0:T(8,128)(2,1)} %refs_6_.1), custom_call_target="tpu_custom_call" | custom-call | flops 4000000000 | bytes 4194304 | tf_op jit(solution)/shard_map/block/pallas_call | solution.py:592
  37.9 1.0 %copy.9 = bf16[4,8,128,128]{3,2,1,0:T(8,128)(2,1)} copy(bf16[4,8,128,128]{3,2,1,0:T(8,128)(2,1)S(1)} %block.1) | data formatting | bytes 2097152

commit v5 on v4

--- a/solution.py
+++ b/solution.py
@@ -464,8 +464,9 @@
     halo3 = halo_copies(3, xin, 0, 2)
     halo4 = halo_copies(4, hid, 0, 2)
     send_halo(halo0)
+    send_cross(0, xin, (0, 1))
     send_halo(halo5)
-    send_cross(0, xin, (0, 1, 2))
+    send_cross(0, xin, (2,))
 
     for load in weight_loads:
         load.wait()
@@ -482,7 +483,6 @@
     for part in range(PARTS):
         spatial(w1, s1, 4, part)
     pass_relay(0, xin, (5,))
-    pass_edges(0, xin, halo3, relayed)
     activate_pair(xin, 2, pair01, halo5)
     for part in range(PARTS):
         spatial(w1, s1, 2, part)
@@ -490,6 +490,8 @@
     send_first(1, hid)
     send_halo(halo1)
     send_cross(1, hid, (0, 1))
+
+    pass_edges(0, xin, halo3, relayed)
 
     parts = []
     earlier(0, xin, w1, s1, gain_first, halo3, lambda part: parts.append(hidden_part(2, part)))

time: 38.9 us -> 38.9 us (level)
  the two profiles are of different devices: /device:TPU:32 before, /device:TPU:25 now
where the time goes in v5:
time: 38.9 us; the launch traced here: 38.6 us
  Pallas kernels  37.6 us (97%)
  local copies, waits for them, and re-layouts  0.97 us (2%)
    pallas_call x1, Pallas kernels, shards(): call(*[pltpu.with_memory_space_constraint(x, pltpu.HBM) for x in inputs])  37.6 us
    unnamed x1, local copies, waits for them, and re-layouts  0.97 us

profile of v5, /device:TPU:25, one launch (start us, length us, event | category | flops | bytes accessed | tf_op | source)
XLA Modules:
  0.0 38.6 jit_solution(17849816795605901061)
XLA Ops:
  0.0 37.6 %block.1 = bf16[4,8,128,128]{3,2,1,0:T(8,128)(2,1)S(1)} custom-call(bf16[4,8,128,128]{3,2,1,0:T(8,128)(2,1)} %refs_0_.1, f32[128]{0:T(128)} %refs_1_.1, bf16[9,128,128]{2,1,0:T(8,128)(2,1)} %refs_2_.1, bf16[3,128,128]{2,1,0:T(8,128)(2,1)} %refs_3_.1, f32[128]{0:T(128)} %refs_4_.1, bf16[9,128,128]{2,1,0:T(8,128)(2,1)} %refs_5_.1, bf16[3,128,128]{2,1,0:T(8,128)(2,1)} %refs_6_.1), custom_call_target="tpu_custom_call" | custom-call | flops 4000000000 | bytes 4194304 | tf_op jit(solution)/shard_map/block/pallas_call | solution.py:594
  37.6 1.0 %copy.9 = bf16[4,8,128,128]{3,2,1,0:T(8,128)(2,1)} copy(bf16[4,8,128,128]{3,2,1,0:T(8,128)(2,1)S(1)} %block.1) | data formatting | bytes 2097152
